TPU v7x, 32 devices: a whole 2x2x4 slice. The times are simulated.
32 devices in a mesh: lat: 4 (over x, core), lon: 2 (over y), ch: 4 (over z).
Axes of the slice: x: 2, y: 2, z: 4, core: 2. Of those that a mesh axis runs over, the one named last changes fastest.
Arguments:
- grid_field: bfloat16 [1440, 4, 49152], P('lon', 'ch', 'lat'), may hold values from -6 to 6
- first_weight: bfloat16 [4, 2, 96, 96], P('ch'), may hold values from -0.4375 to 0.4375
- first_bias: float32 [4, 2, 96], P('ch'), may hold values from -3 to 3
- second_weight: bfloat16 [4, 2, 96, 96], P('ch'), may hold values from -0.4375 to 0.4375
- second_bias: float32 [4, 2, 96], P('ch'), may hold values from -3 to 3
Outputs:
- mixed: bfloat16 [1440, 4, 49152], P('lon', 'ch', 'lat')
All inputs are finite; a program needn't handle non-finite values.
Results may differ from a plain program's by a relative error of at most 0.0073.
Values may be sent and summed in bfloat16 or wider, within the bound.
A program may use at most 256 MiB of HBM per device.

v0:
```python
import math

import jax
import jax.numpy as jnp
from jax import lax
from jax.sharding import PartitionSpec as P

shrink_level = 0.01


def phase_tables(length):
    indices = jnp.arange(length, dtype=jnp.int32)
    product = indices[:, None] * indices[None, :] % length
    angles = product.astype(jnp.float32) * (2.0 * math.pi / length)
    return (jnp.cos(angles), jnp.sin(angles))


def lon_tables(length):
    cosine_tab, sine_tab = phase_tables(length)
    kept_modes = length // 2
    factor = 1.0 / math.sqrt(length)
    forward = jnp.concatenate([cosine_tab[:kept_modes], -sine_tab[:kept_modes]], axis=0) * factor
    weights = jnp.where(jnp.arange(kept_modes) == 0, 1.0, 2.0).astype(jnp.float32)
    inverse = (
        jnp.concatenate(
            [cosine_tab[:, :kept_modes] * weights, -sine_tab[:, :kept_modes] * weights], axis=1
        )
        * factor
    )
    return (forward.astype(jnp.bfloat16), inverse.astype(jnp.bfloat16))


def lat_tables(length):
    cosine_tab, sine_tab = phase_tables(length)
    factor = 1.0 / math.sqrt(length)
    forward = (
        jnp.stack(
            [jnp.stack([cosine_tab, sine_tab], axis=1), jnp.stack([-sine_tab, cosine_tab], axis=1)],
            axis=0,
        )
        * factor
    )
    inverse = (
        jnp.stack(
            [jnp.stack([cosine_tab, -sine_tab], axis=1), jnp.stack([sine_tab, cosine_tab], axis=1)],
            axis=0,
        )
        * factor
    )
    return (forward.astype(jnp.bfloat16), inverse.astype(jnp.bfloat16))


def complex_blocks(weight):
    real_part, imag_part = (weight[:, 0], weight[:, 1])
    return jnp.stack(
        [jnp.stack([real_part, imag_part], axis=2), jnp.stack([-imag_part, real_part], axis=2)],
        axis=1,
    )


def block_mixing(mode_data, first_weight, first_bias, second_weight, second_bias):
    shape = mode_data.shape
    blocks_here = first_weight.shape[0]
    block_width = first_weight.shape[2]
    split_data = mode_data.reshape(shape[0], shape[1], shape[2], blocks_here, block_width)
    hidden = jnp.einsum(
        "rkqbc,brcsd->skqbd",
        split_data,
        complex_blocks(first_weight),
        preferred_element_type=jnp.float32,
    )
    hidden = jax.nn.relu(hidden + jnp.moveaxis(first_bias, 1, 0)[:, None, None, :, :]).astype(
        jnp.bfloat16
    )
    output = jnp.einsum(
        "rkqbc,brcsd->skqbd",
        hidden,
        complex_blocks(second_weight),
        preferred_element_type=jnp.float32,
    )
    output = output + jnp.moveaxis(second_bias, 1, 0)[:, None, None, :, :]
    shrunk = jnp.sign(output) * jnp.maximum(jnp.abs(output) - shrink_level, 0.0)
    return shrunk.astype(jnp.bfloat16).reshape(shape)


def lat_apply(data, table):
    local_lat = data.shape[2]
    own_rows = lax.dynamic_slice_in_dim(table, lax.axis_index("lat") * local_lat, local_lat, 1)
    result = jnp.einsum(
        "sqrh,rkhc->skqc",
        own_rows,
        lax.all_gather(data, "lat", axis=2, tiled=True),
        preferred_element_type=jnp.float32,
    )
    return result.astype(jnp.bfloat16)


def per_device(grid_field, first_weight, first_bias, second_weight, second_bias):
    lon_devices = lax.axis_size("lon")
    lat_devices = lax.axis_size("lat")
    block_width = first_weight.shape[2]
    local_lon, blocks_here, merged = grid_field.shape
    local_lat = merged // block_width
    local_chan = blocks_here * block_width
    lon_size = local_lon * lon_devices
    lat_size = local_lat * lat_devices
    kept_modes = lon_size // 2
    lon_forward, lon_inverse = lon_tables(lon_size)
    lat_forward, lat_inverse = lat_tables(lat_size)
    reordered = grid_field.reshape(local_lon, blocks_here, local_lat, block_width).transpose(
        0, 2, 1, 3
    )
    flattened = reordered.reshape(local_lon, local_lat * local_chan)
    gathered = lax.all_to_all(flattened, "lon", split_axis=1, concat_axis=0, tiled=True)
    spectra = jnp.dot(lon_forward, gathered, preferred_element_type=jnp.float32).astype(
        jnp.bfloat16
    )
    spectra = spectra.reshape(2, kept_modes, gathered.shape[1])
    spectra = lax.all_to_all(spectra, "lon", split_axis=1, concat_axis=2, tiled=True)
    spectra = spectra.reshape(2, spectra.shape[1], local_lat, local_chan)
    mode_data = lat_apply(spectra, lat_forward)
    shrunk = block_mixing(mode_data, first_weight, first_bias, second_weight, second_bias)
    returned = lat_apply(shrunk, lat_inverse)
    returned = returned.reshape(2, returned.shape[1], local_lat * local_chan)
    returned = lax.all_to_all(returned, "lon", split_axis=2, concat_axis=1, tiled=True)
    columns = returned.reshape(2 * kept_modes, returned.shape[2])
    grid_out = jnp.dot(lon_inverse, columns, preferred_element_type=jnp.float32) + gathered.astype(
        jnp.float32
    )
    grid_out = lax.all_to_all(
        grid_out.astype(jnp.bfloat16), "lon", split_axis=0, concat_axis=1, tiled=True
    )
    grid_out = grid_out.reshape(local_lon, local_lat, blocks_here, block_width).transpose(
        0, 2, 1, 3
    )
    return grid_out.reshape(grid_field.shape)


def solution(mesh):
    in_specs = (
        P("lon", "ch", "lat"),
        P("ch", None, None, None),
        P("ch", None, None),
        P("ch", None, None, None),
        P("ch", None, None),
    )
    out_specs = P("lon", "ch", "lat")
    return jax.shard_map(
        per_device, mesh=mesh, in_specs=in_specs, out_specs=out_specs, check_vma=False
    )
```

profile of v0, /device:TPU:0, one launch (start us, length us, event | category | flops | bytes accessed | tf_op | source)
XLA Modules:
  0.0 2259.5 jit_solution(452647109507282424)
XLA Ops:
  6.5 27.5 %all_to_all.48 = bf16[720,2,6144]{2,1,0:T(2,128)(2,1)} reshape(bf16[720,1,12288]{2,0,1:T(8,128)(2,1)} %param.5) | data formatting | bytes 35389440 | tf_op jit(solution)/shard_map/all_to_all | solution.py:114
  34.0 19.5 copy.64
  53.5 10.0 all-to-all-start
  63.5 0.0 all-gather.4.cloned.1.call-start
  63.6 37.0 %fusion.27 = (f32[1440,1440]{1,0:T(8,128)S(1)}, f32[1440,1440]{1,0:T(8,128)S(1)}) fusion(), kind=kLoop, calls=%fused_computation.31 | loop fusion | flops 18662400 | bytes 16588800 | tf_op jit(solution)/shard_map/sin | solution.py:15
  100.5 0.0 copy-start.1
  100.6 0.0 copy-start
  100.6 3.4 copy-done.1
  104.0 3.1 slice.34
  107.1 0.9 copy-done
  108.0 2.5 slice_negate_fusion
  110.5 146.6 %all-to-all-done = bf16[720,2,6144]{2,0,1:T(8,128)(2,1)} async-done(((bf16[720,2,6144]{2,0,1:T(8,128)(2,1)}), bf16[720,2,6144]{2,0,1:T(8,128)(2,1)}, u32[]{:S(2)}, u32[]{:S(2)}) %all-to-all-start) | async-done | bytes 17694752 | tf_op jit(solution)/shard_map/all_to_all | solution.py:114
  257.1 35.2 %convolution_convert_fusion = bf16[1440,6144]{1,0:T(8,128)(2,1)} fusion(bf16[1440,6144]{1,0:T(8,128)(2,1)} %bitcast.17, f32[720,1440]{1,0:T(8,128)} %slice_negate_fusion, f32[720,1440]{1,0:T(8,128)} %slice.34), kind=kOutput, calls=%fused_computation.12 | convolution fusion | flops 25495465984 | bytes 43683840 | tf_op jit(solution)/shard_map/dot_general | solution.py:115
  292.2 89.8 %copy.65 = bf16[2,720,6144]{2,0,1:T(2,128)(2,1)S(1)} copy(bf16[2,720,6144]{2,1,0:T(8,128)(2,1)} %bitcast.163) | data formatting | bytes 35389440 | tf_op jit(solution)/shard_map/reshape | solution.py:118
  382.1 197.5 %all_to_all.65 = bf16[2,720,6144]{2,0,1:T(2,128)(2,1)} all-to-all(bf16[2,720,6144]{2,0,1:T(2,128)(2,1)S(1)} %copy.65), channel_id=1, replica_groups=mesh['lat'=4,'lon'=2,'ch'=4] {'lon'}, dimensions={1} | all-to-all | bytes 35389440 | tf_op jit(solution)/shard_map/all_to_all | solution.py:119
  579.6 19.4 copy.66
  599.1 24.1 %copy.67 = bf16[2,360,2,6144]{1,3,2,0:T(8,128)(2,1)} copy(bf16[2,360,2,6144]{3,1,2,0:T(8,128)(2,1)} %bitcast.159) | data formatting | bytes 35389440 | tf_op jit(solution)/shard_map/all_to_all | solution.py:119
  623.2 26.3 %copy.68 = bf16[2,360,128,96]{2,3,0,1:T(8,128)(2,1)} copy(bf16[2,360,128,96]{1,3,2,0:T(8,128)(2,1)} %bitcast.157) | data formatting | bytes 35389440 | tf_op jit(solution)/shard_map/reshape | solution.py:120
  649.5 0.0 all-gather.4.cloned.1.call-update
  649.5 0.0 copy-start.4
  649.5 0.2 all-gather.6.cloned.1.call-start
  649.7 0.5 copy-done.2
  650.3 0.1 copy.91
  650.4 0.1 copy.90
  650.5 0.0 copy-done.3
  650.5 0.1 copy.89
  650.6 0.1 copy.88
  650.8 3.9 fusion.63
  654.7 4.1 fusion.58
  658.8 5.1 fusion.40
  663.8 411.0 %all-gather.4.cloned.1.call-done = bf16[2,360,512,96]{2,3,0,1:T(8,128)(2,1)} async-done(((bf16[2,360,128,96]{2,3,0,1:T(8,128)(2,1)}), bf16[2,360,512,96]{2,3,0,1:T(8,128)(2,1)}) %all-gather.4.cloned.1.call-update) | async-done | bytes 70778896 | tf_op jit(solution)/shard_map/all_gather | solution.py:92
  1074.9 0.0 copy-done.4
  1074.9 36.0 %fusion.10 = bf16[2,360,128,96]{2,3,1,0:T(8,128)(2,1)} fusion(f32[2,96]{1,0:T(2,128)S(1)} %bitcast.168, bf16[2,360,512,96]{2,3,0,1:T(8,128)(2,1)} %all-gather.4.cloned.1.call-done, s32[]{:T(128)S(6)} %select_n.65, f32[1,512,2,512]{3,1,2,0:T(8,128)} %get-tuple-element.6, f32[1,512,2,512]{3,1,2,0:T(8,128)} %get-tuple-element.9, ...), kind=kOutput, calls=%fused_computation.16 | convolution fusion | flops 21553102848 | bytes 92742400 | tf_op jit(solution)/shard_map/rkqbc,brcsd->skqbd/dot_general | solution.py:66
  1110.9 0.0 copy-done.5
  1110.9 24.4 %fusion.6 = bf16[2,360,128,1,96]{2,4,1,0,3:T(8,128)(2,1)} fusion(f32[2,96]{1,0:T(2,128)S(1)} %bitcast.169, bf16[2,360,128,96]{2,3,1,0:T(8,128)(2,1)} %fusion.10, bf16[1,1,96,2,96]{2,4,1,3,0:T(8,128)(2,1)S(1)} %get-tuple-element.16, bf16[1,1,96,2,96]{2,4,1,3,0:T(8,128)(2,1)S(1)} %get-tuple-element.15), kind=kOutput, calls=%fused_computation.13 | convolution fusion | flops 3459465216 | bytes 35463936 | tf_op jit(solution)/shard_map/rkqbc,brcsd->skqbd/dot_general | solution.py:75
  1135.3 0.0 all-gather.6.cloned.1.call-update
  1135.3 425.2 %all-gather.6.cloned.1.call-done = bf16[2,360,512,1,96]{2,4,1,0,3:T(8,128)(2,1)} async-done(((bf16[2,360,128,1,96]{2,4,1,0,3:T(8,128)(2,1)}), bf16[2,360,512,1,96]{2,4,1,0,3:T(8,128)(2,1)}) %all-gather.6.cloned.1.call-update) | async-done | bytes 70778896 | tf_op jit(solution)/shard_map/all_gather | solution.py:92
  1560.5 33.8 %fusion.11 = bf16[2,360,128,96]{2,3,0,1:T(8,128)(2,1)} fusion(s32[]{:T(128)S(6)} %select_n.65, f32[1,512,2,512]{3,1,2,0:T(8,128)} %get-tuple-element.10, f32[1,512,2,512]{3,1,2,0:T(8,128)S(1)} %get-tuple-element.5, bf16[2,360,512,1,96]{2,4,1,0,3:T(8,128)(2,1)} %all-gather.6.cloned.1.call-done), kind=kOutput, calls=%fused_computation.17 | convolution fusion | flops 18129027072 | bytes 92667904 | tf_op jit(solution)/shard_map/sqrh,rkhc->skqc/dot_general | solution.py:89
  1594.4 26.6 %copy.71 = bf16[2,360,128,96]{1,3,2,0:T(8,128)(2,1)} copy(bf16[2,360,128,96]{2,3,0,1:T(8,128)(2,1)} %fusion.11) | data formatting | bytes 35389440 | tf_op jit(solution)/shard_map/convert_element_type | solution.py:95
  1620.9 34.8 %copy.72 = bf16[2,360,12288]{1,0,2:T(2,128)(2,1)} copy(bf16[2,360,12288]{1,2,0:T(8,128)(2,1)} %bitcast.158) | data formatting | bytes 35389440 | tf_op jit(solution)/shard_map/reshape | solution.py:124
  1655.7 10.5 all-to-all-start.2
  1666.2 7.8 slice_multiply_fusion
  1674.0 197.6 %all-to-all-done.2 = bf16[2,360,12288]{1,0,2:T(2,128)(2,1)} async-done(((bf16[2,360,12288]{1,0,2:T(2,128)(2,1)}), bf16[2,360,12288]{1,0,2:T(2,128)(2,1)}, u32[]{:S(2)}, u32[]{:S(2)}) %all-to-all-start.2) | async-done | bytes 17694752 | tf_op jit(solution)/shard_map/all_to_all | solution.py:125
  1871.6 45.6 %copy.74 = bf16[2,2,360,6144]{3,2,1,0:T(8,128)(2,1)} copy(bf16[2,2,360,6144]{2,0,3,1:T(2,128)(2,1)} %bitcast.54) | data formatting | bytes 35389440 | tf_op jit(solution)/shard_map/all_to_all | solution.py:125
  1917.2 36.9 %add_convert_fusion = bf16[1440,6144]{1,0:T(8,128)(2,1)} fusion(bf16[1440,6144]{1,0:T(8,128)(2,1)} %bitcast.17, bf16[1440,6144]{1,0:T(8,128)(2,1)} %bitcast.161, f32[1440,720]{1,0:T(8,128)} %get-tuple-element.20, f32[1440,720]{1,0:T(8,128)} %get-tuple-element.19), kind=kOutput, calls=%fused_computation.11 | convolution fusion | flops 25513160704 | bytes 61378560 | tf_op jit(solution)/shard_map/dot_general | solution.py:127
  1954.1 197.9 %all_to_all.66 = bf16[2,720,6144]{2,1,0:T(8,128)(2,1)S(1)} all-to-all(bf16[2,720,6144]{2,1,0:T(8,128)(2,1)} %bitcast.162), channel_id=1, replica_groups=mesh['lat'=4,'lon'=2,'ch'=4] {'lon'}, dimensions={0} | all-to-all | bytes 35389440 | tf_op jit(solution)/shard_map/all_to_all | solution.py:130
  2152.0 72.4 %copy.75 = bf16[720,2,6144]{2,1,0:T(2,128)(2,1)} copy(bf16[720,2,6144]{2,0,1:T(8,128)(2,1)S(1)} %bitcast.160) | data formatting | bytes 35389440 | tf_op jit(solution)/shard_map/all_to_all | solution.py:130
  2224.4 28.1 %reshape_transpose_reshape.4 = bf16[720,1,12288]{2,0,1:T(8,128)(2,1)} reshape(bf16[720,2,6144]{2,1,0:T(2,128)(2,1)} %copy.75) | data formatting | bytes 35389440 | tf_op jit(solution)/shard_map/reshape;transpose;reshape | solution.py:136
  (10 shorter events, 0.1 us)
Async XLA Ops:
  53.5 203.6 %all-to-all-start = ((bf16[720,2,6144]{2,0,1:T(8,128)(2,1)}), bf16[720,2,6144]{2,0,1:T(8,128)(2,1)}, u32[]{:S(2)}, u32[]{:S(2)}) async-start(bf16[720,2,6144]{2,0,1:T(8,128)(2,1)} %copy.64), calls=%async_computation | async-start | bytes 35389440 | tf_op jit(solution)/shard_map/all_to_all | solution.py:114
  63.5 1011.3 %all-gather.4.cloned.1.call-start = ((), (), s32[]{:S(2)}) async-start(), calls=%async_computation.4 | async-start | bytes 88473600 | tf_op jit(solution)/shard_map/all_gather | solution.py:92
  100.5 3.4 copy-start.1
  100.6 7.4 copy-start
  649.5 0.8 copy-start.2
  649.5 1.0 copy-start.3
  649.5 425.4 %copy-start.4 = (f32[1,2,96]{2,1,0:T(2,128)S(1)}, f32[1,2,96]{2,1,0:T(2,128)}, u32[]{:S(2)}) copy-start(f32[1,2,96]{2,1,0:T(2,128)} %param.7) | copy-start | bytes 2308
  649.5 911.0 %all-gather.6.cloned.1.call-start = ((), (), s32[]{:S(2)}) async-start(), calls=%async_computation.5 | async-start | bytes 88473600 | tf_op jit(solution)/shard_map/all_gather | solution.py:92
  1074.9 36.0 %copy-start.5 = (f32[1,2,96]{2,1,0:T(2,128)S(1)}, f32[1,2,96]{2,1,0:T(2,128)}, u32[]{:S(2)}) copy-start(f32[1,2,96]{2,1,0:T(2,128)} %param.9) | copy-start | bytes 2308
  1655.7 215.9 %all-to-all-start.2 = ((bf16[2,360,12288]{1,0,2:T(2,128)(2,1)}), bf16[2,360,12288]{1,0,2:T(2,128)(2,1)}, u32[]{:S(2)}, u32[]{:S(2)}) async-start(bf16[2,360,12288]{1,0,2:T(2,128)(2,1)} %copy.72), calls=%async_computation.2 | async-start | bytes 37748736 | tf_op jit(solution)/shard_map/all_to_all | solution.py:125
Sparse Core Ops, SparseCore 0:
  649.6 425.1 all-gather.3
  1135.5 424.9 all-gather.5
where the time goes:
time: 2270 us; the launch traced here: 2260 us
  waiting for transfers between devices  1180 us (52%)
  local copies, waits for them, and re-layouts  423 us (19%)
  blocking collectives  395 us (17%)
  matrix products  166 us (7%)
  other arithmetic  60.3 us (3%)
    all_gather x2, waiting for transfers between devices, lat_apply(): lax.all_gather(data, 'lat', axis=2, tiled=True)  836 us
    all_to_all x1, blocking collectives, per_device(): lax.all_to_all(grid_out.astype(jnp.bfloat16), 'lon', split_axis=0, concat...  198 us
    all_to_all x1, waiting for transfers between devices, per_device(): lax.all_to_all(returned, 'lon', split_axis=2, concat_axis=1, tiled=True)  198 us
    all_to_all x1, blocking collectives, per_device(): lax.all_to_all(spectra, 'lon', split_axis=1, concat_axis=2, tiled=True)  198 us
    all_to_all x1, waiting for transfers between devices, per_device(): lax.all_to_all(flattened, 'lon', split_axis=1, concat_axis=0, tiled=True)  147 us
    reshape x1, local copies, waits for them, and re-layouts, per_device(): spectra = spectra.reshape(2, kept_modes, gathered.shape[1])  89.8 us
    all_to_all x1, local copies, waits for them, and re-layouts, per_device(): lax.all_to_all(grid_out.astype(jnp.bfloat16), 'lon', split_axis=0, concat...  72.4 us
    all_to_all x2, local copies, waits for them, and re-layouts, per_device(): lax.all_to_all(flattened, 'lon', split_axis=1, concat_axis=0, tiled=True)  47 us
  transfers between devices with their start and end apart: 4, of which 4 were waited for; matrix products, arithmetic and copies ran while one was open for 3% of the time, Pallas kernels for 0%

commit v1 on v0

v1 whole, which is shorter than its diff:
```python
import math

import jax
import jax.numpy as jnp
import ml_dtypes
import numpy as np
from jax import lax
from jax.sharding import PartitionSpec as P

shrink_level = 0.01
row_chunks = 2
mode_chunks = 2
group = ("lat", "lon")


def phase_tables(length):
    indices = np.arange(length, dtype=np.int64)
    product = indices[:, None] * indices[None, :] % length
    angles = product.astype(np.float32) * np.float32(2.0 * math.pi / length)
    return np.cos(angles), np.sin(angles)


def chunk_sizes(modes):
    fours = -(-modes // 4)
    parts = min(mode_chunks, fours)
    return [4 * (fours * (i + 1) // parts - fours * i // parts) for i in range(parts)]


def lon_tables(length, owners, sizes, modes, lon_devices):
    cosine, sine = phase_tables(length)
    kept = length // 2
    local = length // lon_devices
    factor = np.float32(1.0 / math.sqrt(length))
    weights = np.where(np.arange(kept) == 0, 1.0, 2.0).astype(np.float32)[:, None]
    forward = np.stack([cosine[:kept], -sine[:kept]]) * factor
    inverse = np.stack([cosine[:kept] * weights, -sine[:kept] * weights]) * factor
    result = []
    start = 0
    for size in sizes:
        both = []
        for table in (forward, inverse):
            rows = np.zeros((owners, 2, size, length), np.float32)
            for owner in range(owners):
                low = owner * modes + start
                high = min(low + size, (owner + 1) * modes, kept)
                if high > low:
                    rows[owner, :, : high - low] = table[:, low:high]
            both.append(rows.reshape(owners, 2 * size, lon_devices, local))
        result.append(
            (
                both[0].transpose(0, 2, 1, 3).astype(ml_dtypes.bfloat16),
                both[1].transpose(2, 0, 3, 1).astype(ml_dtypes.bfloat16),
            )
        )
        start += size
    return result


def lat_tables(length):
    cosine, sine = phase_tables(length)
    factor = np.float32(1.0 / math.sqrt(length))
    forward = np.stack([np.stack([cosine, sine], 1), np.stack([-sine, cosine], 1)], 0) * factor
    inverse = np.stack([np.stack([cosine, -sine], 1), np.stack([sine, cosine], 1)], 0) * factor
    return forward.astype(ml_dtypes.bfloat16), inverse.astype(ml_dtypes.bfloat16)


def complex_blocks(weight):
    real_part, imag_part = (weight[:, 0], weight[:, 1])
    return jnp.stack(
        [jnp.stack([real_part, imag_part], axis=2), jnp.stack([-imag_part, real_part], axis=2)],
        axis=1,
    )


def block_mixing(mode_data, first_weight, first_bias, second_weight, second_bias):
    shape = mode_data.shape
    blocks_here = first_weight.shape[0]
    block_width = first_weight.shape[2]
    split_data = mode_data.reshape(shape[0], shape[1], shape[2], blocks_here, block_width)
    hidden = jnp.einsum(
        "rkqbc,brcsd->skqbd",
        split_data,
        complex_blocks(first_weight),
        preferred_element_type=jnp.float32,
    )
    hidden = jax.nn.relu(hidden + jnp.moveaxis(first_bias, 1, 0)[:, None, None, :, :]).astype(
        jnp.bfloat16
    )
    output = jnp.einsum(
        "rkqbc,brcsd->skqbd",
        hidden,
        complex_blocks(second_weight),
        preferred_element_type=jnp.float32,
    )
    output = output + jnp.moveaxis(second_bias, 1, 0)[:, None, None, :, :]
    shrunk = jnp.sign(output) * jnp.maximum(jnp.abs(output) - shrink_level, 0.0)
    return shrunk.astype(jnp.bfloat16).reshape(shape)


def partner_permute(value, axes, count, step):
    return lax.ppermute(value, axes, [(i, i ^ step) for i in range(count)])


def per_device(grid_field, first_weight, first_bias, second_weight, second_bias):
    lon_devices = lax.axis_size("lon")
    lat_devices = lax.axis_size("lat")
    owners = lon_devices * lat_devices
    block_width = first_weight.shape[2]
    local_lon, blocks_here, merged = grid_field.shape
    local_lat = merged // block_width
    lon_size = local_lon * lon_devices
    lat_size = local_lat * lat_devices
    modes = -(-(lon_size // 2) // owners)
    sizes = chunk_sizes(modes)
    lon_chunks = lon_tables(lon_size, owners, sizes, modes, lon_devices)
    lat_forward, lat_inverse = lat_tables(lat_size)

    assert blocks_here == 1
    lon_index = lax.axis_index("lon")
    me = lax.axis_index("lat") * lon_devices + lon_index
    pairwise = owners <= 8 and owners & (owners - 1) == 0
    order = [(me ^ s) if pairwise else s for s in range(owners)]
    lon_order = [lon_index ^ t for t in range(lon_devices)]

    def exchange(pieces):
        if pairwise:
            return [
                partner_permute(piece, group, owners, s) if s else piece
                for s, piece in enumerate(pieces)
            ]
        joined = lax.all_to_all(
            jnp.concatenate(pieces, axis=0), group, split_axis=0, concat_axis=0, tiled=True
        )
        return jnp.split(joined, owners, axis=0)

    own_rows = local_lat // lon_devices
    own_columns = own_rows * block_width
    chunk_columns = own_columns // row_chunks
    flat = grid_field.reshape(local_lon, merged)

    def field_piece(owner, chunk):
        return lax.dynamic_slice(
            flat, (0, owner * own_columns + chunk * chunk_columns), (local_lon, chunk_columns)
        )

    gathered = []
    for c in range(row_chunks):
        pieces = [
            partner_permute(field_piece(lon_order[t], c), "lon", lon_devices, t)
            if t
            else field_piece(lon_index, c)
            for t in range(lon_devices)
        ]
        gathered.append(jnp.concatenate(pieces, axis=0))

    def pick(table, indices, axis):
        table = jnp.asarray(table)
        return [lax.dynamic_index_in_dim(table, i, axis, keepdims=False) for i in indices]

    forward_tables = []
    inverse_tables = []
    for forward, inverse in lon_chunks:
        rows = jnp.concatenate(pick(forward, order, 0), axis=1)
        forward_tables.append(jnp.concatenate(pick(rows, lon_order, 0), axis=1))
        halves = pick(inverse, lon_order, 0)
        inverse_tables.append([jnp.concatenate(pick(half, order, 0), axis=1) for half in halves])
    inverse_tables = [
        jnp.concatenate([chunk[t] for chunk in inverse_tables], axis=1) for t in range(lon_devices)
    ]

    def row_blocks(table, axis):
        table = jnp.asarray(table)
        return jnp.concatenate(
            [lax.dynamic_slice_in_dim(table, i * own_rows, own_rows, axis) for i in order],
            axis=axis,
        )

    lat_forward = row_blocks(lat_forward, 3)
    lat_inverse = row_blocks(lat_inverse, 1)

    returned_pieces = []
    for size, table in zip(sizes, forward_tables):
        received = []
        for c in range(row_chunks):
            spectra = jnp.dot(table, gathered[c], preferred_element_type=jnp.float32).astype(
                jnp.bfloat16
            )
            received.append(exchange(jnp.split(spectra, owners, axis=0)))
        data = jnp.concatenate(
            [received[c][s] for s in range(owners) for c in range(row_chunks)], axis=1
        )
        data = data.reshape(2, size, lat_size, block_width)
        mode_data = jnp.einsum(
            "sqrh,rkhc->skqc", lat_forward, data, preferred_element_type=jnp.float32
        ).astype(jnp.bfloat16)
        shrunk = block_mixing(mode_data, first_weight, first_bias, second_weight, second_bias)
        returned = jnp.einsum(
            "shrq,rkqc->skhc", lat_inverse, shrunk, preferred_element_type=jnp.float32
        ).astype(jnp.bfloat16)
        returned = returned.reshape(2 * size, lat_size * block_width)
        by_chunk = []
        for c in range(row_chunks):
            starts = [s * own_columns + c * chunk_columns for s in range(owners)]
            by_chunk.append(exchange([returned[:, a : a + chunk_columns] for a in starts]))
        returned_pieces.append(by_chunk)

    out = jnp.zeros((local_lon, merged), jnp.bfloat16)
    for c in range(row_chunks):
        columns = jnp.concatenate(
            [piece for by_chunk in returned_pieces for piece in by_chunk[c]], axis=0
        )
        for t in reversed(range(lon_devices)):
            field_rows = gathered[c][t * local_lon : (t + 1) * local_lon]
            mixed = jnp.dot(inverse_tables[t], columns, preferred_element_type=jnp.float32)
            mixed = (mixed + field_rows.astype(jnp.float32)).astype(jnp.bfloat16)
            if t:
                mixed = partner_permute(mixed, "lon", lon_devices, t)
            start = lon_order[t] * own_columns + c * chunk_columns
            out = lax.dynamic_update_slice(out, mixed, (0, start))
    return out.reshape(grid_field.shape)


def solution(mesh):
    in_specs = (
        P("lon", "ch", "lat"),
        P("ch", None, None, None),
        P("ch", None, None),
        P("ch", None, None, None),
        P("ch", None, None),
    )
    out_specs = P("lon", "ch", "lat")
    return jax.shard_map(
        per_device, mesh=mesh, in_specs=in_specs, out_specs=out_specs, check_vma=False
    )
```

time: 2270 us -> 1080 us (0.48)
  waiting for transfers between devices: 1180 us -> 571 us
  blocking collectives: 395 us -> 0 us
  local copies, waits for them, and re-layouts: 423 us -> 273 us
  other arithmetic: 60.3 us -> 0.06 us
  starting transfers between devices: 20.8 us -> 53.2 us
    all_gather x2 -> x0, waiting for transfers between devices: 836 us -> none  [lat_apply(): lax.all_gather(data, 'lat', axis=2, tiled=True)]
    ppermute x0 -> x60, waiting for transfers between devices: none -> 571 us  [partner_permute(): return lax.ppermute(value, axes, [(i, i ^ step) for i in range(count)])]
    all_to_all x2 -> x0, blocking collectives: 395 us -> none  [the longest x1 198 us: per_device(): lax.all_to_all(grid_out.astype(jnp.bfloat16), 'lon', split_axis=0, concat...]
    all_to_all x2 -> x0, waiting for transfers between devices: 344 us -> none  [the longest x1 198 us: per_device(): lax.all_to_all(returned, 'lon', split_axis=2, concat_axis=1, tiled=True)]
    all_to_all x6 -> x0, local copies, waits for them, and re-layouts: 209 us -> none  [the longest x1 72.4 us: per_device(): lax.all_to_all(grid_out.astype(jnp.bfloat16), 'lon', split_axis=0, concat...]
    unnamed x16 -> x163, local copies, waits for them, and re-layouts: 5.25 us -> 88 us
    reshape x3 -> x5, local copies, waits for them, and re-layouts: 151 us -> 74.2 us  [the longest x2 39 us: per_device(): returned = returned.reshape(2 * size, lat_size * block_width)]
    ppermute x0 -> x60, starting transfers between devices: none -> 53.2 us  [partner_permute(): return lax.ppermute(value, axes, [(i, i ^ step) for i in range(count)])]
  transfers between devices with their start and end apart: 4 -> 60, of which waited for: 4 -> 34; matrix products, arithmetic and copies ran while one was open for 3% -> 38% of each run, Pallas kernels for 0% -> 0%
where the time goes in v1:
time: 1080 us; the launch traced here: 1060 us
  waiting for transfers between devices  571 us (53%)
  local copies, waits for them, and re-layouts  273 us (25%)
  matrix products  166 us (15%)
  starting transfers between devices  53.2 us (5%)
    ppermute x60, waiting for transfers between devices, partner_permute(): return lax.ppermute(value, axes, [(i, i ^ step) for i in range(count)])  571 us
    unnamed x163, local copies, waits for them, and re-layouts  88 us
    ppermute x60, starting transfers between devices, partner_permute(): return lax.ppermute(value, axes, [(i, i ^ step) for i in range(count)])  53.2 us
    dot_general x4, matrix products, per_device(): jnp.dot(inverse_tables[t], columns, preferred_element_type=jnp.float32)  47.1 us
    reshape x2, local copies, waits for them, and re-layouts, per_device(): returned = returned.reshape(2 * size, lat_size * block_width)  39 us
    dot_general x4, matrix products, per_device(): jnp.dot(table, gathered[c], preferred_element_type=jnp.float32)  36.8 us
    dot_general x2, matrix products, block_mixing(): jnp.einsum('rkqbc,brcsd->skqbd', split_data, complex_blocks(first_weight)...  33.2 us
    reshape x2, local copies, waits for them, and re-layouts, per_device(): data = data.reshape(2, size, lat_size, block_width)  33.1 us
  transfers between devices with their start and end apart: 60, of which 34 were waited for; matrix products, arithmetic and copies ran while one was open for 38% of the time, Pallas kernels for 0%

profile of v1, /device:TPU:0, one launch (start us, length us, event | category | flops | bytes accessed | tf_op | source)
XLA Modules:
  0.0 1064.6 jit_solution(3963318243588353051)
XLA Ops:
  0.0 13.0 %dynamic-slice_bitcast_fusion.1 = (bf16[720,3072]{1,0:T(8,128)(2,1)}, bf16[720,3072]{1,0:T(8,128)(2,1)}, bf16[720,3072]{1,0:T(8,128)(2,1)}, bf16[720,3072]{1,0:T(8,128)(2,1)}) fusion(bf16[720,1,12288]{2,0,1:T(8,128)(2,1)} %param.11, s32[]{:T(128)S(6)} %select_n.173, s32[]{:T(128)S(6)} %select_n.172, s32[]{:T(128)S(6)} %select_n.171, s32[]{:T(128)S(6)} %select_n.174), kind=kLoop, calls=%fused_computation.57 | loop fusion | bytes 35389456 | tf_op jit(solution)/shard_map/dynamic_slice | solution.py:142
  29.8 16.2 %concatenate.48 = bf16[2,512,2,512]{3,2,1,0:T(2,128)(2,1)S(1)} concatenate(bf16[2,512,2,64]{3,2,1,0:T(2,128)(2,1)} %get-tuple-element.115, bf16[2,512,2,64]{3,2,1,0:T(2,128)(2,1)} %get-tuple-element.114, bf16[2,512,2,64]{3,2,1,0:T(2,128)(2,1)} %get-tuple-element.113, bf16[2,512,2,64]{3,2,1,0:T(2,128)(2,1)} %get-tuple-element.112, bf16[2,512,2,64]{3,2,1,0:T(2,128)(2,1)} %get-tuple-element.111, ...), dimensions={3} | concatenate | bytes 4194304 | tf_op jit(solution)/shard_map/concatenate | solution.py:173
  70.4 42.1 %collective-permute-done = bf16[720,3072]{1,0:T(8,128)(2,1)} collective-permute-done((bf16[720,3072]{1,0:T(8,128)(2,1)}, bf16[720,3072]{1,0:T(8,128)(2,1)}, u32[]{:S(2)}, u32[]{:S(2)}) %collective-permute-start) | collective-permute-done | bytes 4423712 | tf_op jit(solution)/shard_map/ppermute | solution.py:101
  112.6 8.9 fusion.60
  124.9 82.5 %collective-permute-done.1 = bf16[720,3072]{1,0:T(8,128)(2,1)} collective-permute-done((bf16[720,3072]{1,0:T(8,128)(2,1)}, bf16[720,3072]{1,0:T(8,128)(2,1)}, u32[]{:S(2)}, u32[]{:S(2)}) %collective-permute-start.1) | collective-permute-done | bytes 4423712 | tf_op jit(solution)/shard_map/ppermute | solution.py:101
  207.4 8.8 fusion.61
  220.2 9.6 fusion.54
  231.9 9.4 fusion.55
  263.0 10.7 %collective-permute-done.9 = bf16[88,3072]{1,0:T(8,128)(2,1)S(1)} collective-permute-done((bf16[88,3072]{1,0:T(8,128)(2,1)S(1)}, bf16[88,3072]{1,0:T(8,128)(2,1)S(1)}, u32[]{:S(2)}, u32[]{:S(2)}) %collective-permute-start.9) | collective-permute-done | bytes 540704 | tf_op jit(solution)/shard_map/ppermute | solution.py:101
  274.6 10.1 collective-permute-done.10
  286.4 9.9 collective-permute-done.11
  308.9 10.2 collective-permute-done.13
  321.2 9.6 collective-permute-done.14
  332.1 9.7 collective-permute-done.15
  344.1 16.0 %reshape.181 = bf16[2,44,512,96,1]{3,2,1,0,4:T(8,128)(2,1)} reshape(bf16[88,49152]{1,0:T(8,128)(2,1)} %constant_dynamic-update-slice_fusion) | data formatting | bytes 17301504 | tf_op jit(solution)/shard_map/reshape | solution.py:192
  360.2 16.3 %fusion.23 = bf16[2,44,512,96]{2,3,1,0:T(8,128)(2,1)} fusion(f32[2,96]{1,0:T(2,128)S(1)} %bitcast.301, bf16[2,512,2,512,1]{1,3,2,0,4:T(8,128)(2,1)S(1)} %copy-done.4, bf16[2,44,512,96,1]{3,2,1,0,4:T(8,128)(2,1)} %reshape.181, bf16[1,1,96,2,96]{2,4,1,3,0:T(8,128)(2,1)S(1)} %get-tuple-element.124, bf16[1,1,96,2,96]{2,4,1,3,0:T(8,128)(2,1)S(1)} %get-tuple-element.123), kind=kOutput, calls=%fused_computation.37 | convolution fusion | flops 10536763392 | bytes 19473152 | tf_op jit(solution)/shard_map/rkqbc,brcsd->skqbd/dot_general | solution.py:80
  376.5 12.2 %fusion.19 = bf16[2,44,512,96,1]{2,3,1,0,4:T(8,128)(2,1)S(1)} fusion(f32[2,96]{1,0:T(2,128)S(1)} %bitcast.303, bf16[2,44,512,96]{2,3,1,0:T(8,128)(2,1)} %fusion.23, bf16[1,1,96,2,96]{2,4,1,3,0:T(8,128)(2,1)S(1)} %get-tuple-element.122, bf16[1,1,96,2,96]{2,4,1,3,0:T(8,128)(2,1)S(1)} %get-tuple-element.121), kind=kOutput, calls=%fused_computation.34 | convolution fusion | flops 1691369472 | bytes 17376000 | tf_op jit(solution)/shard_map/rkqbc,brcsd->skqbd/dot_general | solution.py:89
  388.6 11.3 %fusion.24 = bf16[2,44,512,96]{2,3,0,1:T(8,128)(2,1)} fusion(bf16[2,44,512,96,1]{2,3,1,0,4:T(8,128)(2,1)S(1)} %fusion.19, bf16[2,512,2,512]{3,1,2,0:T(8,128)(2,1)S(1)} %copy-done.28), kind=kOutput, calls=%fused_computation.38 | convolution fusion | flops 8862695424 | bytes 19398656 | tf_op jit(solution)/shard_map/shrq,rkqc->skhc/dot_general | solution.py:197
  399.9 13.9 %copy.30 = bf16[2,44,512,96]{3,2,1,0:T(8,128)(2,1)} copy(bf16[2,44,512,96]{2,3,0,1:T(8,128)(2,1)} %fusion.24) | data formatting | bytes 17301504 | tf_op jit(solution)/shard_map/convert_element_type | solution.py:199
  413.9 18.7 %reshape.172 = bf16[88,49152]{1,0:T(8,128)(2,1)} reshape(bf16[2,44,512,96]{3,2,1,0:T(8,128)(2,1)} %copy.30) | data formatting | bytes 17301504 | tf_op jit(solution)/shard_map/reshape | solution.py:200
  459.2 11.4 %collective-permute-done.30 = bf16[96,3072]{1,0:T(8,128)(2,1)S(1)} collective-permute-done((bf16[96,3072]{1,0:T(8,128)(2,1)S(1)}, bf16[96,3072]{1,0:T(8,128)(2,1)S(1)}, u32[]{:S(2)}, u32[]{:S(2)}) %collective-permute-start.30) | collective-permute-done | bytes 589856 | tf_op jit(solution)/shard_map/ppermute | solution.py:101
  472.9 10.9 %collective-permute-done.31 = bf16[96,3072]{1,0:T(8,128)(2,1)S(1)} collective-permute-done((bf16[96,3072]{1,0:T(8,128)(2,1)S(1)}, bf16[96,3072]{1,0:T(8,128)(2,1)S(1)}, u32[]{:S(2)}, u32[]{:S(2)}) %collective-permute-start.31) | collective-permute-done | bytes 589856 | tf_op jit(solution)/shard_map/ppermute | solution.py:101
  485.3 11.1 %collective-permute-done.32 = bf16[96,3072]{1,0:T(8,128)(2,1)S(1)} collective-permute-done((bf16[96,3072]{1,0:T(8,128)(2,1)S(1)}, bf16[96,3072]{1,0:T(8,128)(2,1)S(1)}, u32[]{:S(2)}, u32[]{:S(2)}) %collective-permute-start.32) | collective-permute-done | bytes 589856 | tf_op jit(solution)/shard_map/ppermute | solution.py:101
  498.2 9.1 collective-permute-done.33
  509.6 10.3 collective-permute-done.34
  522.9 11.2 %collective-permute-done.35 = bf16[96,3072]{1,0:T(8,128)(2,1)S(1)} collective-permute-done((bf16[96,3072]{1,0:T(8,128)(2,1)S(1)}, bf16[96,3072]{1,0:T(8,128)(2,1)S(1)}, u32[]{:S(2)}, u32[]{:S(2)}) %collective-permute-start.35) | collective-permute-done | bytes 589856 | tf_op jit(solution)/shard_map/ppermute | solution.py:101
  536.5 10.3 collective-permute-done.36
  549.0 17.1 %reshape.193 = bf16[2,48,512,96,1]{3,2,1,0,4:T(8,128)(2,1)} reshape(bf16[96,49152]{1,0:T(8,128)(2,1)} %constant_dynamic-update-slice_fusion.14) | data formatting | bytes 18874368 | tf_op jit(solution)/shard_map/reshape | solution.py:192
  566.0 16.9 %fusion.12 = bf16[2,48,512,96]{2,3,1,0:T(8,128)(2,1)} fusion(f32[2,96]{1,0:T(2,128)S(1)} %bitcast.302, bf16[2,512,2,512,1]{1,3,2,0,4:T(8,128)(2,1)S(1)} %copy-done.4, bf16[2,48,512,96,1]{3,2,1,0,4:T(8,128)(2,1)} %reshape.193, bf16[1,1,96,2,96]{2,4,1,3,0:T(8,128)(2,1)S(1)} %get-tuple-element.124, bf16[1,1,96,2,96]{2,4,1,3,0:T(8,128)(2,1)S(1)} %get-tuple-element.123), kind=kOutput, calls=%fused_computation.21 | convolution fusion | flops 11494637568 | bytes 21046016 | tf_op jit(solution)/shard_map/rkqbc,brcsd->skqbd/dot_general | solution.py:80
  582.9 13.1 %fusion.8 = bf16[2,48,512,96,1]{2,3,1,0,4:T(8,128)(2,1)S(1)} fusion(f32[2,96]{1,0:T(2,128)S(1)} %bitcast.304, bf16[2,48,512,96]{2,3,1,0:T(8,128)(2,1)} %fusion.12, bf16[1,1,96,2,96]{2,4,1,3,0:T(8,128)(2,1)S(1)} %get-tuple-element.122, bf16[1,1,96,2,96]{2,4,1,3,0:T(8,128)(2,1)S(1)} %get-tuple-element.121), kind=kOutput, calls=%fused_computation.18 | convolution fusion | flops 1845116928 | bytes 18948864 | tf_op jit(solution)/shard_map/rkqbc,brcsd->skqbd/dot_general | solution.py:89
  596.0 12.4 %fusion.13 = bf16[2,48,512,96]{2,3,0,1:T(8,128)(2,1)} fusion(bf16[2,48,512,96,1]{2,3,1,0,4:T(8,128)(2,1)S(1)} %fusion.8, bf16[2,512,2,512]{3,1,2,0:T(8,128)(2,1)S(1)} %copy-done.29), kind=kOutput, calls=%fused_computation.22 | convolution fusion | flops 9668395008 | bytes 20971520 | tf_op jit(solution)/shard_map/shrq,rkqc->skhc/dot_general | solution.py:197
  608.5 14.7 %copy.33 = bf16[2,48,512,96]{3,2,1,0:T(8,128)(2,1)} copy(bf16[2,48,512,96]{2,3,0,1:T(8,128)(2,1)} %fusion.13) | data formatting | bytes 18874368 | tf_op jit(solution)/shard_map/convert_element_type | solution.py:199
  623.2 20.3 %reshape.176 = bf16[96,49152]{1,0:T(8,128)(2,1)} reshape(bf16[2,48,512,96]{3,2,1,0:T(8,128)(2,1)} %copy.33) | data formatting | bytes 18874368 | tf_op jit(solution)/shard_map/reshape | solution.py:200
  659.7 11.3 %collective-permute-done.22 = bf16[88,3072]{1,0:T(8,128)(2,1)S(1)} collective-permute-done((bf16[88,3072]{1,0:T(8,128)(2,1)}, bf16[88,3072]{1,0:T(8,128)(2,1)S(1)}, u32[]{:S(2)}, u32[]{:S(2)}) %collective-permute-start.22) | collective-permute-done | bytes 540704 | tf_op jit(solution)/shard_map/ppermute | solution.py:101
  680.9 17.1 %collective-permute-done.47 = bf16[88,3072]{1,0:T(8,128)(2,1)S(1)} collective-permute-done((bf16[88,3072]{1,0:T(8,128)(2,1)S(1)}, bf16[88,3072]{1,0:T(8,128)(2,1)S(1)}, u32[]{:S(2)}, u32[]{:S(2)}) %collective-permute-start.47) | collective-permute-done | bytes 540704 | tf_op jit(solution)/shard_map/ppermute | solution.py:101
  705.3 12.0 %collective-permute-done.51 = bf16[88,3072]{1,0:T(8,128)(2,1)S(1)} collective-permute-done((bf16[88,3072]{1,0:T(8,128)(2,1)S(1)}, bf16[88,3072]{1,0:T(8,128)(2,1)S(1)}, u32[]{:S(2)}, u32[]{:S(2)}) %collective-permute-start.51) | collective-permute-done | bytes 540704 | tf_op jit(solution)/shard_map/ppermute | solution.py:101
  743.3 31.7 %collective-permute-done.39 = bf16[96,3072]{1,0:T(8,128)(2,1)S(1)} collective-permute-done((bf16[96,3072]{1,0:T(8,128)(2,1)}, bf16[96,3072]{1,0:T(8,128)(2,1)S(1)}, u32[]{:S(2)}, u32[]{:S(2)}) %collective-permute-start.39) | collective-permute-done | bytes 589856 | tf_op jit(solution)/shard_map/ppermute | solution.py:101
  778.4 13.9 %collective-permute-done.41 = bf16[96,3072]{1,0:T(8,128)(2,1)S(1)} collective-permute-done((bf16[96,3072]{1,0:T(8,128)(2,1)}, bf16[96,3072]{1,0:T(8,128)(2,1)S(1)}, u32[]{:S(2)}, u32[]{:S(2)}) %collective-permute-start.41) | collective-permute-done | bytes 589856 | tf_op jit(solution)/shard_map/ppermute | solution.py:101
  793.1 9.8 collective-permute-done.42
  804.3 12.6 %collective-permute-done.43 = bf16[96,3072]{1,0:T(8,128)(2,1)S(1)} collective-permute-done((bf16[96,3072]{1,0:T(8,128)(2,1)S(1)}, bf16[96,3072]{1,0:T(8,128)(2,1)S(1)}, u32[]{:S(2)}, u32[]{:S(2)}) %collective-permute-start.43) | collective-permute-done | bytes 589856 | tf_op jit(solution)/shard_map/ppermute | solution.py:101
  817.9 13.3 %add_convert_fusion.3 = bf16[720,3072]{1,0:T(8,128)(2,1)} fusion(bf16[720,3072]{1,0:T(8,128)(2,1)} %collective-permute-done, bf16[720,1472]{1,0:T(8,128)(2,1)S(1)} %concatenate.42, bf16[1472,3072]{1,0:T(8,128)(2,1)} %constant_dynamic-update-slice_fusion.28), kind=kOutput, calls=%fused_computation.33 | convolution fusion | flops 6518292480 | bytes 20011008 | tf_op jit(solution)/shard_map/dot_general | solution.py:214
  842.9 10.7 %collective-permute-done.57 = bf16[96,3072]{1,0:T(8,128)(2,1)S(1)} collective-permute-done((bf16[96,3072]{1,0:T(8,128)(2,1)S(1)}, bf16[96,3072]{1,0:T(8,128)(2,1)S(1)}, u32[]{:S(2)}, u32[]{:S(2)}) %collective-permute-start.57) | collective-permute-done | bytes 589856 | tf_op jit(solution)/shard_map/ppermute | solution.py:101
  853.6 14.0 %collective-permute-done.58 = bf16[96,3072]{1,0:T(8,128)(2,1)S(1)} collective-permute-done((bf16[96,3072]{1,0:T(8,128)(2,1)S(1)}, bf16[96,3072]{1,0:T(8,128)(2,1)S(1)}, u32[]{:S(2)}, u32[]{:S(2)}) %collective-permute-start.58) | collective-permute-done | bytes 589856 | tf_op jit(solution)/shard_map/ppermute | solution.py:101
  867.7 12.2 %add_convert_fusion.1 = bf16[720,3072]{1,0:T(8,128)(2,1)} fusion(bf16[720,3072]{1,0:T(8,128)(2,1)} %collective-permute-done.1, bf16[720,1472]{1,0:T(8,128)(2,1)S(1)} %concatenate.42, bf16[1472,3072]{1,0:T(8,128)(2,1)S(1)} %constant_dynamic-update-slice_fusion.42), kind=kOutput, calls=%fused_computation.31 | convolution fusion | flops 6518292480 | bytes 20011008 | tf_op jit(solution)/shard_map/dot_general | solution.py:214
  883.7 66.4 %collective-permute-done.44 = bf16[720,3072]{1,0:T(8,128)(2,1)} collective-permute-done((bf16[720,3072]{1,0:T(8,128)(2,1)}, bf16[720,3072]{1,0:T(8,128)(2,1)}, u32[]{:S(2)}, u32[]{:S(2)}) %collective-permute-start.44) | collective-permute-done | bytes 4423712 | tf_op jit(solution)/shard_map/ppermute | solution.py:101
  955.3 11.6 %bitcast_dynamic-update-slice_fusion.2 = bf16[720,1,12288]{2,0,1:T(8,128)(2,1)S(1)} fusion(bf16[720,1,12288]{2,0,1:T(8,128)(2,1)S(1)} %bitcast_dynamic-update-slice_fusion.3, s32[]{:T(128)S(6)} %select_n.171, bf16[720,1472]{1,0:T(8,128)(2,1)S(1)} %concatenate.54, bf16[1472,3072]{1,0:T(8,128)(2,1)} %constant_dynamic-update-slice_fusion.28, ...), kind=kOutput, calls=%fused_computation.54 | convolution fusion | flops 6518292480 | bytes 20103172 | tf_op jit(solution)/shard_map/dot_general | solution.py:214
  966.9 78.0 %collective-permute-done.59 = bf16[720,3072]{1,0:T(8,128)(2,1)} collective-permute-done((bf16[720,3072]{1,0:T(8,128)(2,1)}, bf16[720,3072]{1,0:T(8,128)(2,1)}, u32[]{:S(2)}, u32[]{:S(2)}) %collective-permute-start.59) | collective-permute-done | bytes 4423712 | tf_op jit(solution)/shard_map/ppermute | solution.py:101
  1054.1 10.0 bitcast_dynamic-update-slice_fusion
  (291 shorter events, 231.1 us)
Async XLA Ops:
  13.0 99.6 %collective-permute-start = (bf16[720,3072]{1,0:T(8,128)(2,1)}, bf16[720,3072]{1,0:T(8,128)(2,1)}, u32[]{:S(2)}, u32[]{:S(2)}) collective-permute-start(bf16[720,3072]{1,0:T(8,128)(2,1)} %get-tuple-element.6), channel_id=1, source_target_pairs={{0,4},{4,0},{1,5},{5,1},{2,6},{6,2},{3,7},{7,3},{8,12},{12,8},{9,1... | collective-permute-start | bytes 13271048 | tf_op jit(solution)/shard_map/ppermute | solution.py:101
  16.0 191.4 %collective-permute-start.1 = (bf16[720,3072]{1,0:T(8,128)(2,1)}, bf16[720,3072]{1,0:T(8,128)(2,1)}, u32[]{:S(2)}, u32[]{:S(2)}) collective-permute-start(bf16[720,3072]{1,0:T(8,128)(2,1)} %get-tuple-element.8), channel_id=1, source_target_pairs={{0,4},{4,0},{1,5},{5,1},{2,6},{6,2},{3,7},{7,3},{8,12},{12,8},{9,1... | collective-permute-start | bytes 13271048 | tf_op jit(solution)/shard_map/ppermute | solution.py:101
  122.8 120.5 %collective-permute-start.2 = (bf16[88,3072]{1,0:T(8,128)(2,1)}, bf16[88,3072]{1,0:T(8,128)(2,1)}, u32[]{:S(2)}, u32[]{:S(2)}) collective-permute-start(bf16[88,3072]{1,0:T(8,128)(2,1)} %get-tuple-element.71), channel_id=1, source_target_pairs={{0,4},{4,0},{8,12},{12,8},{16,20},{20,16},{24,28},{28,24},{1,5},{5... | collective-permute-start | bytes 1622024 | tf_op jit(solution)/shard_map/ppermute | solution.py:101
  217.6 29.4 %collective-permute-start.3 = (bf16[88,3072]{1,0:T(8,128)(2,1)}, bf16[88,3072]{1,0:T(8,128)(2,1)}, u32[]{:S(2)}, u32[]{:S(2)}) collective-permute-start(bf16[88,3072]{1,0:T(8,128)(2,1)} %get-tuple-element.63), channel_id=1, source_target_pairs={{0,4},{4,0},{8,12},{12,8},{16,20},{20,16},{24,28},{28,24},{1,5},{5... | collective-permute-start | bytes 1622024 | tf_op jit(solution)/shard_map/ppermute | solution.py:101
  219.7 30.7 %collective-permute-start.4 = (bf16[88,3072]{1,0:T(8,128)(2,1)S(1)}, bf16[88,3072]{1,0:T(8,128)(2,1)}, u32[]{:S(2)}, u32[]{:S(2)}) collective-permute-start(bf16[88,3072]{1,0:T(8,128)(2,1)S(1)} %get-tuple-element.70), channel_id=1, source_target_pairs={{0,8},{4,12},{8,0},{12,4},{16,24},{20,28},{24,16},{28,20},{1,9},{5... | collective-permute-start | bytes 1622024 | tf_op jit(solution)/shard_map/ppermute | solution.py:101
  219.7 33.2 %collective-permute-start.5 = (bf16[88,3072]{1,0:T(8,128)(2,1)S(1)}, bf16[88,3072]{1,0:T(8,128)(2,1)}, u32[]{:S(2)}, u32[]{:S(2)}) collective-permute-start(bf16[88,3072]{1,0:T(8,128)(2,1)S(1)} %get-tuple-element.62), channel_id=1, source_target_pairs={{0,8},{4,12},{8,0},{12,4},{16,24},{20,28},{24,16},{28,20},{1,9},{5... | collective-permute-start | bytes 1622024 | tf_op jit(solution)/shard_map/ppermute | solution.py:101
  220.2 36.0 %collective-permute-start.6 = (bf16[88,3072]{1,0:T(8,128)(2,1)S(1)}, bf16[88,3072]{1,0:T(8,128)(2,1)}, u32[]{:S(2)}, u32[]{:S(2)}) collective-permute-start(bf16[88,3072]{1,0:T(8,128)(2,1)S(1)} %get-tuple-element.69), channel_id=1, source_target_pairs={{0,12},{4,8},{8,4},{12,0},{16,28},{20,24},{24,20},{28,16},{1,13},{... | collective-permute-start | bytes 1622024 | tf_op jit(solution)/shard_map/ppermute | solution.py:101
  252.8 31.9 %collective-permute-start.10 = (bf16[88,3072]{1,0:T(8,128)(2,1)S(1)}, bf16[88,3072]{1,0:T(8,128)(2,1)S(1)}, u32[]{:S(2)}, u32[]{:S(2)}) collective-permute-start(bf16[88,3072]{1,0:T(8,128)(2,1)S(1)} %get-tuple-element.67), channel_id=1, source_target_pairs={{0,20},{4,16},{8,28},{12,24},{16,4},{20,0},{24,12},{28,8},{1,21},{... | collective-permute-start | bytes 1622024 | tf_op jit(solution)/shard_map/ppermute | solution.py:101
  256.2 40.1 %collective-permute-start.11 = (bf16[88,3072]{1,0:T(8,128)(2,1)S(1)}, bf16[88,3072]{1,0:T(8,128)(2,1)S(1)}, u32[]{:S(2)}, u32[]{:S(2)}) collective-permute-start(bf16[88,3072]{1,0:T(8,128)(2,1)S(1)} %get-tuple-element.59), channel_id=1, source_target_pairs={{0,20},{4,16},{8,28},{12,24},{16,4},{20,0},{24,12},{28,8},{1,21},{... | collective-permute-start | bytes 1622024 | tf_op jit(solution)/shard_map/ppermute | solution.py:101
  259.5 48.0 %collective-permute-start.12 = (bf16[88,3072]{1,0:T(8,128)(2,1)S(1)}, bf16[88,3072]{1,0:T(8,128)(2,1)S(1)}, u32[]{:S(2)}, u32[]{:S(2)}) collective-permute-start(bf16[88,3072]{1,0:T(8,128)(2,1)S(1)} %get-tuple-element.66), channel_id=1, source_target_pairs={{0,24},{4,28},{8,16},{12,20},{16,8},{20,12},{24,0},{28,4},{1,25},{... | collective-permute-start | bytes 1622024 | tf_op jit(solution)/shard_map/ppermute | solution.py:101
  262.2 56.9 %collective-permute-start.13 = (bf16[88,3072]{1,0:T(8,128)(2,1)S(1)}, bf16[88,3072]{1,0:T(8,128)(2,1)S(1)}, u32[]{:S(2)}, u32[]{:S(2)}) collective-permute-start(bf16[88,3072]{1,0:T(8,128)(2,1)S(1)} %get-tuple-element.58), channel_id=1, source_target_pairs={{0,24},{4,28},{8,16},{12,20},{16,8},{20,12},{24,0},{28,4},{1,25},{... | collective-permute-start | bytes 1622024 | tf_op jit(solution)/shard_map/ppermute | solution.py:101
  273.7 57.0 %collective-permute-start.14 = (bf16[88,3072]{1,0:T(8,128)(2,1)S(1)}, bf16[88,3072]{1,0:T(8,128)(2,1)S(1)}, u32[]{:S(2)}, u32[]{:S(2)}) collective-permute-start(bf16[88,3072]{1,0:T(8,128)(2,1)S(1)} %get-tuple-element.65), channel_id=1, source_target_pairs={{0,28},{4,24},{8,20},{12,16},{16,12},{20,8},{24,4},{28,0},{1,29},{... | collective-permute-start | bytes 1622024 | tf_op jit(solution)/shard_map/ppermute | solution.py:101
  284.7 57.1 %collective-permute-start.15 = (bf16[88,3072]{1,0:T(8,128)(2,1)S(1)}, bf16[88,3072]{1,0:T(8,128)(2,1)S(1)}, u32[]{:S(2)}, u32[]{:S(2)}) collective-permute-start(bf16[88,3072]{1,0:T(8,128)(2,1)S(1)} %get-tuple-element.57), channel_id=1, source_target_pairs={{0,28},{4,24},{8,20},{12,16},{16,12},{20,8},{24,4},{28,0},{1,29},{... | collective-permute-start | bytes 1622024 | tf_op jit(solution)/shard_map/ppermute | solution.py:101
  296.3 143.2 %collective-permute-start.23 = (bf16[96,3072]{1,0:T(8,128)(2,1)}, bf16[96,3072]{1,0:T(8,128)(2,1)}, u32[]{:S(2)}, u32[]{:S(2)}) collective-permute-start(bf16[96,3072]{1,0:T(8,128)(2,1)} %get-tuple-element.55), channel_id=1, source_target_pairs={{0,4},{4,0},{8,12},{12,8},{16,20},{20,16},{24,28},{28,24},{1,5},{5... | collective-permute-start | bytes 1769480 | tf_op jit(solution)/shard_map/ppermute | solution.py:101
  307.5 134.2 %collective-permute-start.24 = (bf16[96,3072]{1,0:T(8,128)(2,1)}, bf16[96,3072]{1,0:T(8,128)(2,1)}, u32[]{:S(2)}, u32[]{:S(2)}) collective-permute-start(bf16[96,3072]{1,0:T(8,128)(2,1)} %get-tuple-element.47), channel_id=1, source_target_pairs={{0,4},{4,0},{8,12},{12,8},{16,20},{20,16},{24,28},{28,24},{1,5},{5... | collective-permute-start | bytes 1769480 | tf_op jit(solution)/shard_map/ppermute | solution.py:101
  319.1 125.9 %collective-permute-start.25 = (bf16[96,3072]{1,0:T(8,128)(2,1)}, bf16[96,3072]{1,0:T(8,128)(2,1)}, u32[]{:S(2)}, u32[]{:S(2)}) collective-permute-start(bf16[96,3072]{1,0:T(8,128)(2,1)} %get-tuple-element.54), channel_id=1, source_target_pairs={{0,8},{4,12},{8,0},{12,4},{16,24},{20,28},{24,16},{28,20},{1,9},{5... | collective-permute-start | bytes 1769480 | tf_op jit(solution)/shard_map/ppermute | solution.py:101
  330.7 117.0 %collective-permute-start.26 = (bf16[96,3072]{1,0:T(8,128)(2,1)}, bf16[96,3072]{1,0:T(8,128)(2,1)}, u32[]{:S(2)}, u32[]{:S(2)}) collective-permute-start(bf16[96,3072]{1,0:T(8,128)(2,1)} %get-tuple-element.46), channel_id=1, source_target_pairs={{0,8},{4,12},{8,0},{12,4},{16,24},{20,28},{24,16},{28,20},{1,9},{5... | collective-permute-start | bytes 1769480 | tf_op jit(solution)/shard_map/ppermute | solution.py:101
  341.8 109.9 %collective-permute-start.27 = (bf16[96,3072]{1,0:T(8,128)(2,1)}, bf16[96,3072]{1,0:T(8,128)(2,1)}, u32[]{:S(2)}, u32[]{:S(2)}) collective-permute-start(bf16[96,3072]{1,0:T(8,128)(2,1)} %get-tuple-element.53), channel_id=1, source_target_pairs={{0,12},{4,8},{8,4},{12,0},{16,28},{20,24},{24,20},{28,16},{1,13},{... | collective-permute-start | bytes 1769480 | tf_op jit(solution)/shard_map/ppermute | solution.py:101
  445.0 25.6 %collective-permute-start.30 = (bf16[96,3072]{1,0:T(8,128)(2,1)S(1)}, bf16[96,3072]{1,0:T(8,128)(2,1)S(1)}, u32[]{:S(2)}, u32[]{:S(2)}) collective-permute-start(bf16[96,3072]{1,0:T(8,128)(2,1)S(1)} %copy-done.14), channel_id=1, source_target_pairs={{0,16},{4,20},{8,24},{12,28},{16,0},{20,4},{24,8},{28,12},{1,17},{... | collective-permute-start | bytes 1769480 | tf_op jit(solution)/shard_map/ppermute | solution.py:101
  447.7 36.1 %collective-permute-start.31 = (bf16[96,3072]{1,0:T(8,128)(2,1)S(1)}, bf16[96,3072]{1,0:T(8,128)(2,1)S(1)}, u32[]{:S(2)}, u32[]{:S(2)}) collective-permute-start(bf16[96,3072]{1,0:T(8,128)(2,1)S(1)} %copy-done.11), channel_id=1, source_target_pairs={{0,20},{4,16},{8,28},{12,24},{16,4},{20,0},{24,12},{28,8},{1,21},{... | collective-permute-start | bytes 1769480 | tf_op jit(solution)/shard_map/ppermute | solution.py:101
  451.7 44.8 %collective-permute-start.32 = (bf16[96,3072]{1,0:T(8,128)(2,1)S(1)}, bf16[96,3072]{1,0:T(8,128)(2,1)S(1)}, u32[]{:S(2)}, u32[]{:S(2)}) collective-permute-start(bf16[96,3072]{1,0:T(8,128)(2,1)S(1)} %copy-done.12), channel_id=1, source_target_pairs={{0,20},{4,16},{8,28},{12,24},{16,4},{20,0},{24,12},{28,8},{1,21},{... | collective-permute-start | bytes 1769480 | tf_op jit(solution)/shard_map/ppermute | solution.py:101
  455.1 52.1 %collective-permute-start.33 = (bf16[96,3072]{1,0:T(8,128)(2,1)S(1)}, bf16[96,3072]{1,0:T(8,128)(2,1)S(1)}, u32[]{:S(2)}, u32[]{:S(2)}) collective-permute-start(bf16[96,3072]{1,0:T(8,128)(2,1)S(1)} %copy-done.9), channel_id=1, source_target_pairs={{0,24},{4,28},{8,16},{12,20},{16,8},{20,12},{24,0},{28,4},{1,25},{... | collective-permute-start | bytes 1769480 | tf_op jit(solution)/shard_map/ppermute | solution.py:101
  457.9 62.0 %collective-permute-start.34 = (bf16[96,3072]{1,0:T(8,128)(2,1)S(1)}, bf16[96,3072]{1,0:T(8,128)(2,1)S(1)}, u32[]{:S(2)}, u32[]{:S(2)}) collective-permute-start(bf16[96,3072]{1,0:T(8,128)(2,1)S(1)} %copy-done.10), channel_id=1, source_target_pairs={{0,24},{4,28},{8,16},{12,20},{16,8},{20,12},{24,0},{28,4},{1,25},{... | collective-permute-start | bytes 1769480 | tf_op jit(solution)/shard_map/ppermute | solution.py:101
  470.6 63.6 %collective-permute-start.35 = (bf16[96,3072]{1,0:T(8,128)(2,1)S(1)}, bf16[96,3072]{1,0:T(8,128)(2,1)S(1)}, u32[]{:S(2)}, u32[]{:S(2)}) collective-permute-start(bf16[96,3072]{1,0:T(8,128)(2,1)S(1)} %get-tuple-element.49), channel_id=1, source_target_pairs={{0,28},{4,24},{8,20},{12,16},{16,12},{20,8},{24,4},{28,0},{1,29},{... | collective-permute-start | bytes 1769480 | tf_op jit(solution)/shard_map/ppermute | solution.py:101
  483.8 63.0 %collective-permute-start.36 = (bf16[96,3072]{1,0:T(8,128)(2,1)S(1)}, bf16[96,3072]{1,0:T(8,128)(2,1)S(1)}, u32[]{:S(2)}, u32[]{:S(2)}) collective-permute-start(bf16[96,3072]{1,0:T(8,128)(2,1)S(1)} %get-tuple-element.41), channel_id=1, source_target_pairs={{0,28},{4,24},{8,20},{12,16},{16,12},{20,8},{24,4},{28,0},{1,29},{... | collective-permute-start | bytes 1769480 | tf_op jit(solution)/shard_map/ppermute | solution.py:101
  496.4 147.1 %collective-permute-start.16 = (bf16[88,3072]{1,0:T(8,128)(2,1)}, bf16[88,3072]{1,0:T(8,128)(2,1)}, u32[]{:S(2)}, u32[]{:S(2)}) collective-permute-start(bf16[88,3072]{1,0:T(8,128)(2,1)} %get-tuple-element.39), channel_id=1, source_target_pairs={{0,4},{4,0},{8,12},{12,8},{16,20},{20,16},{24,28},{28,24},{1,5},{5... | collective-permute-start | bytes 1622024 | tf_op jit(solution)/shard_map/ppermute | solution.py:101
  507.2 138.8 %collective-permute-start.17 = (bf16[88,3072]{1,0:T(8,128)(2,1)}, bf16[88,3072]{1,0:T(8,128)(2,1)}, u32[]{:S(2)}, u32[]{:S(2)}) collective-permute-start(bf16[88,3072]{1,0:T(8,128)(2,1)} %get-tuple-element.38), channel_id=1, source_target_pairs={{0,8},{4,12},{8,0},{12,4},{16,24},{20,28},{24,16},{28,20},{1,9},{5... | collective-permute-start | bytes 1622024 | tf_op jit(solution)/shard_map/ppermute | solution.py:101
  519.9 130.9 %collective-permute-start.18 = (bf16[88,3072]{1,0:T(8,128)(2,1)}, bf16[88,3072]{1,0:T(8,128)(2,1)}, u32[]{:S(2)}, u32[]{:S(2)}) collective-permute-start(bf16[88,3072]{1,0:T(8,128)(2,1)} %get-tuple-element.37), channel_id=1, source_target_pairs={{0,12},{4,8},{8,4},{12,0},{16,28},{20,24},{24,20},{28,16},{1,13},{... | collective-permute-start | bytes 1622024 | tf_op jit(solution)/shard_map/ppermute | solution.py:101
  534.1 118.9 %collective-permute-start.19 = (bf16[88,3072]{1,0:T(8,128)(2,1)}, bf16[88,3072]{1,0:T(8,128)(2,1)}, u32[]{:S(2)}, u32[]{:S(2)}) collective-permute-start(bf16[88,3072]{1,0:T(8,128)(2,1)} %get-tuple-element.36), channel_id=1, source_target_pairs={{0,16},{4,20},{8,24},{12,28},{16,0},{20,4},{24,8},{28,12},{1,17},{... | collective-permute-start | bytes 1622024 | tf_op jit(solution)/shard_map/ppermute | solution.py:101
  546.8 108.1 %collective-permute-start.20 = (bf16[88,3072]{1,0:T(8,128)(2,1)}, bf16[88,3072]{1,0:T(8,128)(2,1)}, u32[]{:S(2)}, u32[]{:S(2)}) collective-permute-start(bf16[88,3072]{1,0:T(8,128)(2,1)} %get-tuple-element.35), channel_id=1, source_target_pairs={{0,20},{4,16},{8,28},{12,24},{16,4},{20,0},{24,12},{28,8},{1,21},{... | collective-permute-start | bytes 1622024 | tf_op jit(solution)/shard_map/ppermute | solution.py:101
  650.8 27.0 %collective-permute-start.45 = (bf16[88,3072]{1,0:T(8,128)(2,1)}, bf16[88,3072]{1,0:T(8,128)(2,1)S(1)}, u32[]{:S(2)}, u32[]{:S(2)}) collective-permute-start(bf16[88,3072]{1,0:T(8,128)(2,1)} %get-tuple-element.31), channel_id=1, source_target_pairs={{0,4},{4,0},{8,12},{12,8},{16,20},{20,16},{24,28},{28,24},{1,5},{5... | collective-permute-start | bytes 1622024 | tf_op jit(solution)/shard_map/ppermute | solution.py:101
  653.0 25.7 %collective-permute-start.46 = (bf16[88,3072]{1,0:T(8,128)(2,1)S(1)}, bf16[88,3072]{1,0:T(8,128)(2,1)S(1)}, u32[]{:S(2)}, u32[]{:S(2)}) collective-permute-start(bf16[88,3072]{1,0:T(8,128)(2,1)S(1)} %copy-done.24), channel_id=1, source_target_pairs={{0,8},{4,12},{8,0},{12,4},{16,24},{20,28},{24,16},{28,20},{1,9},{5... | collective-permute-start | bytes 1622024 | tf_op jit(solution)/shard_map/ppermute | solution.py:101
  654.9 43.1 %collective-permute-start.47 = (bf16[88,3072]{1,0:T(8,128)(2,1)S(1)}, bf16[88,3072]{1,0:T(8,128)(2,1)S(1)}, u32[]{:S(2)}, u32[]{:S(2)}) collective-permute-start(bf16[88,3072]{1,0:T(8,128)(2,1)S(1)} %copy-done.23), channel_id=1, source_target_pairs={{0,12},{4,8},{8,4},{12,0},{16,28},{20,24},{24,20},{28,16},{1,13},{... | collective-permute-start | bytes 1622024 | tf_op jit(solution)/shard_map/ppermute | solution.py:101
  658.7 40.2 %collective-permute-start.48 = (bf16[88,3072]{1,0:T(8,128)(2,1)S(1)}, bf16[88,3072]{1,0:T(8,128)(2,1)S(1)}, u32[]{:S(2)}, u32[]{:S(2)}) collective-permute-start(bf16[88,3072]{1,0:T(8,128)(2,1)S(1)} %copy-done.22), channel_id=1, source_target_pairs={{0,16},{4,20},{8,24},{12,28},{16,0},{20,4},{24,8},{28,12},{1,17},{... | collective-permute-start | bytes 1622024 | tf_op jit(solution)/shard_map/ppermute | solution.py:101
  671.0 28.6 %collective-permute-start.49 = (bf16[88,3072]{1,0:T(8,128)(2,1)S(1)}, bf16[88,3072]{1,0:T(8,128)(2,1)S(1)}, u32[]{:S(2)}, u32[]{:S(2)}) collective-permute-start(bf16[88,3072]{1,0:T(8,128)(2,1)S(1)} %copy-done.21), channel_id=1, source_target_pairs={{0,20},{4,16},{8,28},{12,24},{16,4},{20,0},{24,12},{28,8},{1,21},{... | collective-permute-start | bytes 1622024 | tf_op jit(solution)/shard_map/ppermute | solution.py:101
  677.8 26.7 %collective-permute-start.50 = (bf16[88,3072]{1,0:T(8,128)(2,1)S(1)}, bf16[88,3072]{1,0:T(8,128)(2,1)S(1)}, u32[]{:S(2)}, u32[]{:S(2)}) collective-permute-start(bf16[88,3072]{1,0:T(8,128)(2,1)S(1)} %copy-done.20), channel_id=1, source_target_pairs={{0,24},{4,28},{8,16},{12,20},{16,8},{20,12},{24,0},{28,4},{1,25},{... | collective-permute-start | bytes 1622024 | tf_op jit(solution)/shard_map/ppermute | solution.py:101
  678.7 38.7 %collective-permute-start.51 = (bf16[88,3072]{1,0:T(8,128)(2,1)S(1)}, bf16[88,3072]{1,0:T(8,128)(2,1)S(1)}, u32[]{:S(2)}, u32[]{:S(2)}) collective-permute-start(bf16[88,3072]{1,0:T(8,128)(2,1)S(1)} %copy-done.19), channel_id=1, source_target_pairs={{0,28},{4,24},{8,20},{12,16},{16,12},{20,8},{24,4},{28,0},{1,29},{... | collective-permute-start | bytes 1622024 | tf_op jit(solution)/shard_map/ppermute | solution.py:101
  731.5 99.7 %collective-permute-start.52 = (bf16[96,3072]{1,0:T(8,128)(2,1)}, bf16[96,3072]{1,0:T(8,128)(2,1)S(1)}, u32[]{:S(2)}, u32[]{:S(2)}) collective-permute-start(bf16[96,3072]{1,0:T(8,128)(2,1)} %get-tuple-element.15), channel_id=1, source_target_pairs={{0,4},{4,0},{8,12},{12,8},{16,20},{20,16},{24,28},{28,24},{1,5},{5... | collective-permute-start | bytes 1769480 | tf_op jit(solution)/shard_map/ppermute | solution.py:101
  733.4 99.5 %collective-permute-start.53 = (bf16[96,3072]{1,0:T(8,128)(2,1)}, bf16[96,3072]{1,0:T(8,128)(2,1)S(1)}, u32[]{:S(2)}, u32[]{:S(2)}) collective-permute-start(bf16[96,3072]{1,0:T(8,128)(2,1)} %get-tuple-element.14), channel_id=1, source_target_pairs={{0,8},{4,12},{8,0},{12,4},{16,24},{20,28},{24,16},{28,20},{1,9},{5... | collective-permute-start | bytes 1769480 | tf_op jit(solution)/shard_map/ppermute | solution.py:101
  733.6 100.9 %collective-permute-start.54 = (bf16[96,3072]{1,0:T(8,128)(2,1)}, bf16[96,3072]{1,0:T(8,128)(2,1)S(1)}, u32[]{:S(2)}, u32[]{:S(2)}) collective-permute-start(bf16[96,3072]{1,0:T(8,128)(2,1)} %get-tuple-element.13), channel_id=1, source_target_pairs={{0,12},{4,8},{8,4},{12,0},{16,28},{20,24},{24,20},{28,16},{1,13},{... | collective-permute-start | bytes 1769480 | tf_op jit(solution)/shard_map/ppermute | solution.py:101
  738.8 36.2 %collective-permute-start.39 = (bf16[96,3072]{1,0:T(8,128)(2,1)}, bf16[96,3072]{1,0:T(8,128)(2,1)S(1)}, u32[]{:S(2)}, u32[]{:S(2)}) collective-permute-start(bf16[96,3072]{1,0:T(8,128)(2,1)} %get-tuple-element.21), channel_id=1, source_target_pairs={{0,12},{4,8},{8,4},{12,0},{16,28},{20,24},{24,20},{28,16},{1,13},{... | collective-permute-start | bytes 1769480 | tf_op jit(solution)/shard_map/ppermute | solution.py:101
  740.8 35.6 %collective-permute-start.40 = (bf16[96,3072]{1,0:T(8,128)(2,1)}, bf16[96,3072]{1,0:T(8,128)(2,1)S(1)}, u32[]{:S(2)}, u32[]{:S(2)}) collective-permute-start(bf16[96,3072]{1,0:T(8,128)(2,1)} %get-tuple-element.20), channel_id=1, source_target_pairs={{0,16},{4,20},{8,24},{12,28},{16,0},{20,4},{24,8},{28,12},{1,17},{... | collective-permute-start | bytes 1769480 | tf_op jit(solution)/shard_map/ppermute | solution.py:101
  776.4 26.5 %collective-permute-start.42 = (bf16[96,3072]{1,0:T(8,128)(2,1)}, bf16[96,3072]{1,0:T(8,128)(2,1)S(1)}, u32[]{:S(2)}, u32[]{:S(2)}) collective-permute-start(bf16[96,3072]{1,0:T(8,128)(2,1)} %get-tuple-element.18), channel_id=1, source_target_pairs={{0,24},{4,28},{8,16},{12,20},{16,8},{20,12},{24,0},{28,4},{1,25},{... | collective-permute-start | bytes 1769480 | tf_op jit(solution)/shard_map/ppermute | solution.py:101
  803.0 31.9 %collective-permute-start.55 = (bf16[96,3072]{1,0:T(8,128)(2,1)}, bf16[96,3072]{1,0:T(8,128)(2,1)S(1)}, u32[]{:S(2)}, u32[]{:S(2)}) collective-permute-start(bf16[96,3072]{1,0:T(8,128)(2,1)} %get-tuple-element.12), channel_id=1, source_target_pairs={{0,16},{4,20},{8,24},{12,28},{16,0},{20,4},{24,8},{28,12},{1,17},{... | collective-permute-start | bytes 1769480 | tf_op jit(solution)/shard_map/ppermute | solution.py:101
  816.9 26.0 %collective-permute-start.56 = (bf16[96,3072]{1,0:T(8,128)(2,1)}, bf16[96,3072]{1,0:T(8,128)(2,1)S(1)}, u32[]{:S(2)}, u32[]{:S(2)}) collective-permute-start(bf16[96,3072]{1,0:T(8,128)(2,1)} %get-tuple-element.11), channel_id=1, source_target_pairs={{0,20},{4,16},{8,28},{12,24},{16,4},{20,0},{24,12},{28,8},{1,21},{... | collective-permute-start | bytes 1769480 | tf_op jit(solution)/shard_map/ppermute | solution.py:101
  832.9 34.7 %collective-permute-start.58 = (bf16[96,3072]{1,0:T(8,128)(2,1)S(1)}, bf16[96,3072]{1,0:T(8,128)(2,1)S(1)}, u32[]{:S(2)}, u32[]{:S(2)}) collective-permute-start(bf16[96,3072]{1,0:T(8,128)(2,1)S(1)} %copy-done.16), channel_id=1, source_target_pairs={{0,28},{4,24},{8,20},{12,16},{16,12},{20,8},{24,4},{28,0},{1,29},{... | collective-permute-start | bytes 1769480 | tf_op jit(solution)/shard_map/ppermute | solution.py:101
  834.6 115.6 %collective-permute-start.44 = (bf16[720,3072]{1,0:T(8,128)(2,1)}, bf16[720,3072]{1,0:T(8,128)(2,1)}, u32[]{:S(2)}, u32[]{:S(2)}) collective-permute-start(bf16[720,3072]{1,0:T(8,128)(2,1)} %add_convert_fusion.3), channel_id=1, source_target_pairs={{0,4},{4,0},{1,5},{5,1},{2,6},{6,2},{3,7},{7,3},{8,12},{12,8},{9,1... | collective-permute-start | bytes 13271048 | tf_op jit(solution)/shard_map/ppermute | solution.py:101
  879.9 164.9 %collective-permute-start.59 = (bf16[720,3072]{1,0:T(8,128)(2,1)}, bf16[720,3072]{1,0:T(8,128)(2,1)}, u32[]{:S(2)}, u32[]{:S(2)}) collective-permute-start(bf16[720,3072]{1,0:T(8,128)(2,1)} %add_convert_fusion.1), channel_id=1, source_target_pairs={{0,4},{4,0},{1,5},{5,1},{2,6},{6,2},{3,7},{7,3},{8,12},{12,8},{9,1... | collective-permute-start | bytes 13271048 | tf_op jit(solution)/shard_map/ppermute | solution.py:101
  (55 other events, 1643.4 us)
